TPU v7x, 32 devices: a whole 2x2x4 slice. The times are simulated.
32 devices in a mesh: groups: 2 (over x), leaf: 16 (over z, y, core).
Axes of the slice: x: 2, y: 2, z: 4, core: 2. Of those that a mesh axis runs over, the one named last changes fastest.
Arguments:
- right_side: float32 [256, 65536], P('groups', 'leaf'), parts along dimension 0, may hold values from -30 to 30
- point_order: int32 [131072], P(('groups', 'leaf')), parts along dimension 0, may hold values from 0 to 65535, as said below
- leaf_blocks: bfloat16 [128, 512, 512], P('leaf'), may hold values from -0.01 to 6, as said below
- bases: bfloat16 [7, 128, 65536], P(None, None, 'leaf'), may hold values from -4 to 4
- rank_weights: float32 [7, 128], replicated, may hold values from 0.05 to 0.6
Outputs:
- field_solution: float32 [256, 65536], P('groups', 'leaf'), parts along dimension 0
- field_residual: float32 [256, 65536], P('groups', 'leaf'), parts along dimension 0
There are 2 independent parts, one for each index of `groups`. A program takes and returns all parts, laid end to end along the dimension named above; an argument that names none is the same for every part. Nothing has to cross between parts.
Inputs may be any that keep to these rules, and one draw needn't show every extreme that they name: `point_order`: each aligned run of 4096 entries holds each of its own 4096 positions once. `leaf_blocks`: every block is symmetric positive definite.
All inputs are finite; a program needn't handle non-finite values.
Results may differ from a plain program's by a relative error of at most 0.0049.
Values sent between devices are 32-bit elements; how exact they have to be, the bound alone decides.
A program may use at most 128 MiB of HBM per device.

v0:
```python
import math
import jax
import jax.numpy as jnp
from jax import lax
from jax.sharding import PartitionSpec as P

ITERS = 2


def from_partner(array, axis, stride):
    return lax.ppermute(array, axis, [(i, i ^ 1 << stride) for i in range(lax.axis_size(axis))])


def scale_level(values, tree_level, rank_weights, leaf_size):
    rank_size = rank_weights.shape[1]
    factor = 1.0 / math.sqrt(rank_size * leaf_size * 2 ** (tree_level + 1))
    return (values * factor * rank_weights[tree_level]).astype(jnp.bfloat16)


def double_up(stacked):
    finished = []
    pending = stacked
    for tree_bit in range(stacked.shape[0]):
        received = from_partner(pending, "leaf", tree_bit)
        pending = pending + received
        finished.append(pending[0])
        pending = pending[1:]
    return finished


def apply_operator(probe, leaf_blocks, bases, rank_weights):
    columns, points = probe.shape
    blocks, leaf_size = (leaf_blocks.shape[0], leaf_blocks.shape[1])
    levels, rank_size = rank_weights.shape
    upper_levels = lax.axis_size("leaf").bit_length() - 1
    local_levels = levels - upper_levels
    probe_tiles = probe.reshape(columns, blocks, leaf_size)
    basis_tiles = bases.reshape(levels, rank_size, blocks, leaf_size)
    dense_part = jnp.einsum(
        "nbj,bjp->nbp", probe_tiles, leaf_blocks, preferred_element_type=jnp.float32
    )
    partial_value = jnp.einsum(
        "nbp,lrbp->blnr", probe_tiles, basis_tiles, preferred_element_type=jnp.float32
    )
    scaled_levels = []
    for tree_level in range(local_levels):
        per_node = 2 ** (tree_level + 1)
        grouped = (
            partial_value[:, tree_level]
            .reshape(blocks // per_node, per_node, columns, rank_size)
            .sum(axis=1)
        )
        scaled = scale_level(grouped, tree_level, rank_weights, leaf_size)
        scaled_levels.append(jnp.repeat(scaled, per_node, axis=0))
    device_terms = partial_value[:, local_levels:].sum(axis=0)
    level_totals = double_up(device_terms)
    for offset_level, level_total in enumerate(level_totals):
        scaled = scale_level(level_total, local_levels + offset_level, rank_weights, leaf_size)
        scaled_levels.append(jnp.broadcast_to(scaled, (blocks, columns, rank_size)))
    stacked = jnp.stack(scaled_levels)
    low_rank = jnp.einsum(
        "lbnr,lrbp->nbp", stacked, basis_tiles, preferred_element_type=jnp.float32
    )
    return (dense_part + low_rank).reshape(columns, points)


def squares(values):
    return lax.psum(jnp.sum(values * values, axis=1), "leaf")


def on_device(right_side, point_order, leaf_blocks, bases, rank_weights):
    columns, points = right_side.shape
    first_point = lax.axis_index("leaf") * points
    local_order = point_order - first_point
    ordered = jnp.take(right_side, local_order, axis=1)
    solution = jnp.zeros_like(ordered)
    residual = ordered
    direction = ordered
    norm_now = squares(residual)
    for iteration in range(ITERS):
        image_field = apply_operator(
            direction.astype(jnp.bfloat16), leaf_blocks, bases, rank_weights
        )
        curvature = lax.psum(jnp.sum(direction * image_field, axis=1), "leaf")
        step_size = norm_now / curvature
        solution = solution + step_size[:, None] * direction
        residual = residual - step_size[:, None] * image_field
        if iteration + 1 < ITERS:
            norm_next = squares(residual)
            direction = residual + (norm_next / norm_now)[:, None] * direction
            norm_now = norm_next
    field_solution = jnp.zeros_like(solution).at[:, local_order].set(solution)
    field_residual = jnp.zeros_like(residual).at[:, local_order].set(residual)
    return (field_solution, field_residual)


def solution(mesh):
    return jax.shard_map(
        on_device,
        mesh=mesh,
        in_specs=(
            P("groups", "leaf"),
            P(("groups", "leaf")),
            P("leaf", None, None),
            P(None, None, "leaf"),
            P(),
        ),
        out_specs=(P("groups", "leaf"), P("groups", "leaf")),
        check_vma=False,
    )
```

profile of v0, /device:TPU:0, one launch (start us, length us, event | category | flops | bytes accessed | tf_op | source)
XLA Modules:
  0.0 227.0 jit_solution(16715418856772773228)
XLA Ops:
  0.6 0.7 compare_and_fusion
  1.4 1.9 copy.14
  3.3 14.2 %gather_fusion = f32[4096,128]{1,0:T(8,128)} fusion(f32[128,4096]{0,1:T(8,128)S(1)} %copy.14, s32[4096]{0:T(1024)S(1)} %broadcast_clamp_fusion), kind=kCustom, calls=%fused_computation | custom fusion | bytes 4210688 | tf_op jit(solution)/shard_map/jit(_take)/gather | solution.py:75
  17.5 1.9 copy.15
  19.4 5.5 %fusion.25 = f32[8,7,128,128]{3,2,1,0:T(8,128)S(1)} fusion(bf16[7,16,8,8,512]{4,3,2,1,0:T(8,128)(2,1)} %bitcast.155, f32[128,8,512]{2,0,1:T(8,128)S(1)} %copy.15, pred[8,512]{1,0:T(8,128)(4,1)S(1)} %broadcast_in_dim.46), kind=kOutput, calls=%fused_computation.41 | convolution fusion | flops 940048384 | bytes 13111296 | tf_op jit(solution)/shard_map/nbp,lrbp->blnr/dot_general | solution.py:42
  25.0 0.1 slice_reduce_fusion.1
  25.1 0.5 collective-permute-start
  25.6 0.1 slice_reduce_fusion.3
  25.7 0.8 copy-done
  26.6 2.1 multiply_reduce_fusion.3
  28.9 0.8 fusion.47
  30.1 3.0 %collective-permute-start.1 = (f32[3,128,128]{2,1,0:T(8,128)S(1)}, f32[3,128,128]{2,1,0:T(8,128)S(1)}, u32[]{:S(2)}, u32[]{:S(2)}) collective-permute-start(f32[3,128,128]{2,1,0:T(8,128)S(1)} %slice.122), channel_id=1, source_target_pairs={{0,2},{1,3},{2,0},{3,1},{4,6},{5,7},{6,4},{7,5},{8,10},{9,11},{10,... | collective-permute-start | bytes 589832 | tf_op jit(solution)/shard_map/ppermute | solution.py:11
  33.2 4.8 %collective-permute-done.1 = f32[3,128,128]{2,1,0:T(8,128)S(1)} collective-permute-done((f32[3,128,128]{2,1,0:T(8,128)S(1)}, f32[3,128,128]{2,1,0:T(8,128)S(1)}, u32[]{:S(2)}, u32[]{:S(2)}) %collective-permute-start.1) | collective-permute-done | bytes 196640 | tf_op jit(solution)/shard_map/ppermute | solution.py:11
  38.0 1.9 collective-permute-start.2
  39.9 3.2 %collective-permute-done.2 = f32[2,128,128]{2,1,0:T(8,128)S(1)} collective-permute-done((f32[2,128,128]{2,1,0:T(8,128)S(1)}, f32[2,128,128]{2,1,0:T(8,128)S(1)}, u32[]{:S(2)}, u32[]{:S(2)}) %collective-permute-start.2) | collective-permute-done | bytes 131104 | tf_op jit(solution)/shard_map/ppermute | solution.py:11
  43.1 2.9 %collective-permute-start.3 = (f32[1,128,128]{2,1,0:T(8,128)S(1)}, f32[1,128,128]{2,1,0:T(8,128)S(1)}, u32[]{:S(2)}, u32[]{:S(2)}) collective-permute-start(f32[1,128,128]{2,1,0:T(8,128)S(1)} %slice.126), channel_id=1, source_target_pairs={{0,8},{1,9},{2,10},{3,11},{4,12},{5,13},{6,14},{7,15},{8,0},{9,1},... | collective-permute-start | bytes 196616 | tf_op jit(solution)/shard_map/ppermute | solution.py:11
  46.0 2.3 %collective-permute-done.3 = f32[1,128,128]{2,1,0:T(8,128)S(1)} collective-permute-done((f32[1,128,128]{2,1,0:T(8,128)S(1)}, f32[1,128,128]{2,1,0:T(8,128)S(1)}, u32[]{:S(2)}, u32[]{:S(2)}) %collective-permute-start.3) | collective-permute-done | bytes 65568 | tf_op jit(solution)/shard_map/ppermute | solution.py:11
  48.5 2.8 %multiply_reduce_fusion.2 = (f32[128]{0:T(128)S(1)}, f32[128,8,512]{2,0,1:T(8,128)}) fusion(f32[128,8,512]{2,0,1:T(8,128)S(1)} %copy.15, pred[8,512]{1,0:T(8,128)(4,1)S(1)} %broadcast_in_dim.46, f32[8,128,512]{2,1,0:T(8,128)S(1)} %fusion.47, bf16[7,8,128,128]{3,2,0,1:T(8,128)(2,1)S(1)} %broadcast_dynamic-update-slice_fusion.5, ...), kind=kOutput, calls=%fused_computation.39 | convolution fusion | flops 941621120 | bytes 15471104 | tf_op jit(solution)/shard_map/lbnr,lrbp->nbp/dot_general | solution.py:61
  51.3 31.1 %all-reduce = (f32[128]{0:T(128)S(1)}, f32[128]{0:T(128)S(1)}) all-reduce(f32[128]{0:T(128)S(1)} %multiply_reduce_fusion.3, f32[128]{0:T(128)S(1)} %get-tuple-element.29), channel_id=1, replica_groups=mesh['groups'=2,'leaf'=16] {'leaf'}, use_global_device_ids=true, to_apply=%region_1.2 | all-reduce | flops 256 | bytes 2048 | tf_op jit(solution)/shard_map/psum | solution.py:68
  82.4 2.1 multiply_reduce_fusion.1
  84.5 29.7 %psum.30 = f32[128]{0:T(128)S(1)} all-reduce(f32[128]{0:T(128)S(1)} %multiply_reduce_fusion.1), channel_id=1, replica_groups=mesh['groups'=2,'leaf'=16] {'leaf'}, use_global_device_ids=true, to_apply=%region_9.10 | all-reduce | flops 128 | bytes 1024 | tf_op jit(solution)/shard_map/psum | solution.py:68
  114.2 2.2 multiply_add_fusion
  116.4 6.3 %fusion.28 = f32[8,7,128,128]{3,2,1,0:T(8,128)S(1)} fusion(bf16[7,16,8,8,512]{4,3,2,1,0:T(8,128)(2,1)} %bitcast.156, f32[128,8,512]{2,0,1:T(8,128)S(1)} %multiply_add_fusion), kind=kOutput, calls=%fused_computation.42 | convolution fusion | flops 940048384 | bytes 13107200 | tf_op jit(solution)/shard_map/nbp,lrbp->blnr/dot_general | solution.py:42
  122.7 0.1 slice_reduce_fusion
  122.8 0.1 slice_reduce_fusion.2
  122.9 2.0 copy-done.6
  124.8 2.0 fusion.45
  127.0 0.7 constant_dynamic-update-slice_fusion.3
  127.9 0.8 constant_dynamic-update-slice_fusion.2
  128.6 1.8 copy.20
  130.5 0.7 broadcast_dynamic-update-slice_fusion.4
  131.4 0.7 broadcast_dynamic-update-slice_fusion.3
  132.1 6.6 %collective-permute-done.5 = f32[3,128,128]{2,1,0:T(8,128)S(1)} collective-permute-done((f32[3,128,128]{2,1,0:T(8,128)S(1)}, f32[3,128,128]{2,1,0:T(8,128)S(1)}, u32[]{:S(2)}, u32[]{:S(2)}) %collective-permute-start.5) | collective-permute-done | bytes 196640 | tf_op jit(solution)/shard_map/ppermute | solution.py:11
  138.7 0.1 collective-permute-start.6
  138.8 5.1 %collective-permute-done.6 = f32[2,128,128]{2,1,0:T(8,128)S(1)} collective-permute-done((f32[2,128,128]{2,1,0:T(8,128)S(1)}, f32[2,128,128]{2,1,0:T(8,128)S(1)}, u32[]{:S(2)}, u32[]{:S(2)}) %collective-permute-start.6) | collective-permute-done | bytes 131104 | tf_op jit(solution)/shard_map/ppermute | solution.py:11
  143.9 0.1 collective-permute-start.7
  144.0 0.7 broadcast_dynamic-update-slice_fusion.2
  144.8 4.8 %collective-permute-done.7 = f32[1,128,128]{2,1,0:T(8,128)S(1)} collective-permute-done((f32[1,128,128]{2,1,0:T(8,128)S(1)}, f32[1,128,128]{2,1,0:T(8,128)S(1)}, u32[]{:S(2)}, u32[]{:S(2)}) %collective-permute-start.7) | collective-permute-done | bytes 65568 | tf_op jit(solution)/shard_map/ppermute | solution.py:11
  149.6 0.7 broadcast_dynamic-update-slice_fusion.1
  150.3 0.7 broadcast_dynamic-update-slice_fusion
  151.1 6.4 %multiply_reduce_fusion = (f32[128]{0:T(128)S(1)}, f32[128,8,512]{2,0,1:T(8,128)}) fusion(f32[128,8,512]{2,0,1:T(8,128)S(1)} %copy-done.3, f32[8,128,512]{2,1,0:T(8,128)S(1)} %copy-done.7, bf16[7,8,128,128]{3,2,0,1:T(8,128)(2,1)} %broadcast_dynamic-update-slice_fusion, bf16[7,16,8,8,512]{4,3,2,1,0:T(8,128)(2,1)} %bitcast.157), kind=kOutput, calls=%fused_computation.34 | convolution fusion | flops 941096832 | bytes 15467008 | tf_op jit(solution)/shard_map/lbnr,lrbp->nbp/dot_general | solution.py:61
  157.4 29.5 %psum.31 = f32[128]{0:T(128)S(1)} all-reduce(f32[128]{0:T(128)S(1)} %get-tuple-element.31), channel_id=1, replica_groups=mesh['groups'=2,'leaf'=16] {'leaf'}, use_global_device_ids=true, to_apply=%region_15.16 | all-reduce | flops 128 | bytes 1024 | tf_op jit(solution)/shard_map/psum | solution.py:84
  186.9 3.1 %copy.21 = f32[128,8,512]{0,2,1:T(8,128)} copy(f32[128,8,512]{2,0,1:T(8,128)} %get-tuple-element.32) | data formatting | bytes 4194304 | tf_op jit(solution)/shard_map/add | solution.py:64
  190.0 3.9 %fusion.14 = (f32[128,4096]{0,1:T(8,128)}, f32[128,4096]{0,1:T(8,128)}) fusion(f32[128,8,512]{0,2,1:T(8,128)} %copy.21, f32[128]{0:T(128)S(1)} %div.11, f32[128,8,512]{0,2,1:T(8,128)} %copy.20, f32[128]{0:T(128)S(1)} %div.9, f32[4096,128]{1,0:T(8,128)S(1)} %copy-done.1, pred[4096]{0:T(1024)(128)(4,1)S(1)} %get-tuple-element.10), kind=kLoop, calls=%fused_computation.20 | loop fusion | flops 2621440 | bytes 10490880 | tf_op jit(solution)/shard_map/sub | solution.py:87
  193.9 12.5 %scatter_custom_fusion.1 = f32[128,4096]{0,1:T(8,128)} fusion(s32[4096]{0:T(1024)S(1)} %get-tuple-element.11, f32[128,4096]{0,1:T(8,128)} %get-tuple-element.8, f32[]{:T(128)} %constant.13.clone.1), kind=kCustom, calls=%fused_computation.17 | custom fusion | bytes 4194308 | tf_op jit(solution)/shard_map/scatter | solution.py:93
  206.4 2.9 %copy.23 = f32[128,4096]{1,0:T(8,128)} copy(f32[128,4096]{0,1:T(8,128)} %scatter_custom_fusion.1) | data formatting | bytes 4194304
  209.3 14.8 %scatter_custom_fusion = f32[128,4096]{0,1:T(8,128)} fusion(s32[4096]{0:T(1024)S(1)} %get-tuple-element.11, f32[128,4096]{0,1:T(8,128)} %get-tuple-element.9, f32[4096,128]{1,0:T(8,128)S(1)} %copy-done.1, f32[128]{0:T(128)S(1)} %div.10, f32[128]{0:T(128)S(1)} %div.11, f32[128]{0:T(128)S(1)} %div.9, f32[]{:T(128)} %constant.18.clone.1, ...), kind=kCustom, calls=%fused_computation.21 | custom fusion | flops 3145728 | bytes 6297096 | tf_op jit(solution)/shard_map/scatter | solution.py:92
  224.1 2.9 %copy.22 = f32[128,4096]{1,0:T(8,128)} copy(f32[128,4096]{0,1:T(8,128)} %scatter_custom_fusion) | data formatting | bytes 4194304
  (70 shorter events, 1.2 us)
Async XLA Ops:
  25.0 1.6 copy-start
  25.1 3.6 %copy-start.8 = (f32[7,128]{1,0:T(8,128)S(1)}, f32[7,128]{1,0:T(8,128)}, u32[]{:S(2)}) copy-start(f32[7,128]{1,0:T(8,128)} %param.9) | copy-start | bytes 10756
  25.1 4.9 %collective-permute-start = (f32[4,128,128]{2,1,0:T(8,128)S(1)}, f32[4,128,128]{2,1,0:T(8,128)S(1)}, u32[]{:S(2)}, u32[]{:S(2)}) collective-permute-start(f32[4,128,128]{2,1,0:T(8,128)S(1)} %slice_reduce_fusion.1), channel_id=1, source_target_pairs={{0,1},{1,0},{2,3},{3,2},{4,5},{5,4},{6,7},{7,6},{8,9},{9,8},{10,11... | collective-permute-start | bytes 786440 | tf_op jit(solution)/shard_map/ppermute | solution.py:11
  26.6 2.4 %copy-start.5 = (bf16[8,512,512]{2,1,0:T(8,128)(2,1)S(1)}, bf16[8,512,512]{2,1,0:T(8,128)(2,1)}, u32[]{:S(2)}) copy-start(bf16[8,512,512]{2,1,0:T(8,128)(2,1)} %param.7) | copy-start | bytes 12582916
  28.9 19.6 %slice-start = ((s8[7340032]{0:T(1024)(128)(4,1)}), s8[4194304]{0:T(1024)(128)(4,1)S(1)}, s32[]{:S(2)}) async-start(s8[7340032]{0:T(1024)(128)(4,1)} %bitcast.158), calls=%async_computation | async-start | bytes 8388608
  28.9 19.6 %slice-start.1 = ((s8[7340032]{0:T(1024)(128)(4,1)}), s8[3145728]{0:T(1024)(128)(4,1)S(1)}, s32[]{:S(2)}) async-start(s8[7340032]{0:T(1024)(128)(4,1)} %bitcast.158), calls=%async_computation.1 | async-start | bytes 6291456
  30.1 7.9 %collective-permute-start.1 = (f32[3,128,128]{2,1,0:T(8,128)S(1)}, f32[3,128,128]{2,1,0:T(8,128)S(1)}, u32[]{:S(2)}, u32[]{:S(2)}) collective-permute-start(f32[3,128,128]{2,1,0:T(8,128)S(1)} %slice.122), channel_id=1, source_target_pairs={{0,2},{1,3},{2,0},{3,1},{4,6},{5,7},{6,4},{7,5},{8,10},{9,11},{10,... | collective-permute-start | bytes 589832 | tf_op jit(solution)/shard_map/ppermute | solution.py:11
  38.0 5.0 %collective-permute-start.2 = (f32[2,128,128]{2,1,0:T(8,128)S(1)}, f32[2,128,128]{2,1,0:T(8,128)S(1)}, u32[]{:S(2)}, u32[]{:S(2)}) collective-permute-start(f32[2,128,128]{2,1,0:T(8,128)S(1)} %slice.124), channel_id=1, source_target_pairs={{0,4},{1,5},{2,6},{3,7},{4,0},{5,1},{6,2},{7,3},{8,12},{9,13},{10,... | collective-permute-start | bytes 393224 | tf_op jit(solution)/shard_map/ppermute | solution.py:11
  43.1 5.2 %collective-permute-start.3 = (f32[1,128,128]{2,1,0:T(8,128)S(1)}, f32[1,128,128]{2,1,0:T(8,128)S(1)}, u32[]{:S(2)}, u32[]{:S(2)}) collective-permute-start(f32[1,128,128]{2,1,0:T(8,128)S(1)} %slice.126), channel_id=1, source_target_pairs={{0,8},{1,9},{2,10},{3,11},{4,12},{5,13},{6,14},{7,15},{8,0},{9,1},... | collective-permute-start | bytes 196616 | tf_op jit(solution)/shard_map/ppermute | solution.py:11
  116.4 6.5 %copy-start.2 = (f32[128,8,512]{2,0,1:T(8,128)}, f32[128,8,512]{2,0,1:T(8,128)S(1)}, u32[]{:S(2)}) copy-start(f32[128,8,512]{2,0,1:T(8,128)S(1)} %multiply_add_fusion) | copy-start | bytes 6291460
  122.7 2.2 copy-start.6
  126.9 1.7 copy-start.4
  126.9 4.3 %collective-permute-start.4 = (f32[4,128,128]{2,1,0:T(8,128)S(1)}, f32[4,128,128]{2,1,0:T(8,128)S(1)}, u32[]{:S(2)}, u32[]{:S(2)}) collective-permute-start(f32[4,128,128]{2,1,0:T(8,128)S(1)} %slice_reduce_fusion), channel_id=1, source_target_pairs={{0,1},{1,0},{2,3},{3,2},{4,5},{5,4},{6,7},{7,6},{8,9},{9,8},{10,11... | collective-permute-start | bytes 786440 | tf_op jit(solution)/shard_map/ppermute | solution.py:11
  131.2 19.9 %copy-start.3 = (f32[128,8,512]{2,0,1:T(8,128)S(1)}, f32[128,8,512]{2,0,1:T(8,128)}, u32[]{:S(2)}) copy-start(f32[128,8,512]{2,0,1:T(8,128)} %copy-done.2) | copy-start | bytes 6291460
  131.2 19.9 %copy-start.7 = (f32[8,128,512]{2,1,0:T(8,128)S(1)}, f32[8,128,512]{2,1,0:T(8,128)}, u32[]{:S(2)}) copy-start(f32[8,128,512]{2,1,0:T(8,128)} %fusion.45) | copy-start | bytes 6291460
  131.3 7.4 %collective-permute-start.5 = (f32[3,128,128]{2,1,0:T(8,128)S(1)}, f32[3,128,128]{2,1,0:T(8,128)S(1)}, u32[]{:S(2)}, u32[]{:S(2)}) collective-permute-start(f32[3,128,128]{2,1,0:T(8,128)S(1)} %slice.132), channel_id=1, source_target_pairs={{0,2},{1,3},{2,0},{3,1},{4,6},{5,7},{6,4},{7,5},{8,10},{9,11},{10,... | collective-permute-start | bytes 589832 | tf_op jit(solution)/shard_map/ppermute | solution.py:11
  138.7 5.2 %collective-permute-start.6 = (f32[2,128,128]{2,1,0:T(8,128)S(1)}, f32[2,128,128]{2,1,0:T(8,128)S(1)}, u32[]{:S(2)}, u32[]{:S(2)}) collective-permute-start(f32[2,128,128]{2,1,0:T(8,128)S(1)} %slice.134), channel_id=1, source_target_pairs={{0,4},{1,5},{2,6},{3,7},{4,0},{5,1},{6,2},{7,3},{8,12},{9,13},{10,... | collective-permute-start | bytes 393224 | tf_op jit(solution)/shard_map/ppermute | solution.py:11
  143.9 5.7 %collective-permute-start.7 = (f32[1,128,128]{2,1,0:T(8,128)S(1)}, f32[1,128,128]{2,1,0:T(8,128)S(1)}, u32[]{:S(2)}, u32[]{:S(2)}) collective-permute-start(f32[1,128,128]{2,1,0:T(8,128)S(1)} %slice.136), channel_id=1, source_target_pairs={{0,8},{1,9},{2,10},{3,11},{4,12},{5,13},{6,14},{7,15},{8,0},{9,1},... | collective-permute-start | bytes 196616 | tf_op jit(solution)/shard_map/ppermute | solution.py:11
  186.9 3.1 %copy-start.1 = (f32[4096,128]{1,0:T(8,128)S(1)}, f32[4096,128]{1,0:T(8,128)}, u32[]{:S(2)}) copy-start(f32[4096,128]{1,0:T(8,128)} %gather_fusion) | copy-start | bytes 6291460
where the time goes:
time: 228 us; the launch traced here: 227 us
  blocking collectives  90.2 us (40%)
  local copies, waits for them, and re-layouts  49.9 us (22%)
  waiting for transfers between devices  26.8 us (12%)
  other arithmetic  26.7 us (12%)
  matrix products  23.8 us (10%)
  starting transfers between devices  8.49 us (4%)
    psum x2, blocking collectives, squares(): return lax.psum(jnp.sum(values * values, axis=1), 'leaf')  60.8 us
    psum x1, blocking collectives, on_device(): curvature = lax.psum(jnp.sum(direction * image_field, axis=1), 'leaf')  29.5 us
    ppermute x8, waiting for transfers between devices, from_partner(): lax.ppermute(array, axis, [(i, i ^ 1 << stride) for i in range(lax.axis_s...  26.8 us
    gather x2, local copies, waits for them, and re-layouts, on_device(): ordered = jnp.take(right_side, local_order, axis=1)  16.1 us
    unnamed x37, local copies, waits for them, and re-layouts  15.3 us
    scatter x1, other arithmetic, on_device(): field_solution = jnp.zeros_like(solution).at[:, local_order].set(solution)  14.8 us
    scatter x1, local copies, waits for them, and re-layouts, on_device(): field_residual = jnp.zeros_like(residual).at[:, local_order].set(residual)  12.5 us
    dot_general x2, matrix products, apply_operator(): jnp.einsum('nbp,lrbp->blnr', probe_tiles, basis_tiles, preferred_element_...  11.8 us
  transfers between devices with their start and end apart: 8, of which 6 were waited for; matrix products, arithmetic and copies ran while one was open for 4% of the time, Pallas kernels for 0%

commit v1 on v0

--- a/solution.py
+++ b/solution.py
@@ -81,7 +81,9 @@
         image_field = apply_operator(
             direction.astype(jnp.bfloat16), leaf_blocks, bases, rank_weights
         )
-        curvature = lax.psum(jnp.sum(direction * image_field, axis=1), "leaf")
+        x = jnp.sum(direction * image_field, axis=1)
+        parts = lax.all_gather(x, "leaf")
+        curvature = jnp.sum(parts, axis=0)
         step_size = norm_now / curvature
         solution = solution + step_size[:, None] * direction
         residual = residual - step_size[:, None] * image_field

time: 228 us -> 245 us (1.075)
  blocking collectives: 90.2 us -> 101 us
  starting transfers between devices: 8.49 us -> 0.95 us
  matrix products: 23.8 us -> 28.7 us
  local copies, waits for them, and re-layouts: 49.9 us -> 54.7 us
  waiting for transfers between devices: 26.8 us -> 31.2 us
    all_gather x0 -> x2, blocking collectives: none -> 34.6 us  [on_device(): parts = lax.all_gather(x, 'leaf')]
    psum x1 -> x0, blocking collectives: 29.5 us -> none  [on_device(): curvature = lax.psum(jnp.sum(direction * image_field, axis=1), 'leaf')]
    ppermute x8, starting transfers between devices: 8.49 us -> 0.95 us  [from_partner(): lax.ppermute(array, axis, [(i, i ^ 1 << stride) for i in range(lax.axis_s...]
    psum x2, blocking collectives: 60.8 us -> 66.5 us  [squares(): return lax.psum(jnp.sum(values * values, axis=1), 'leaf')]
    ppermute x8, waiting for transfers between devices: 26.8 us -> 31.2 us  [from_partner(): lax.ppermute(array, axis, [(i, i ^ 1 << stride) for i in range(lax.axis_s...]
    unnamed x37 -> x35, local copies, waits for them, and re-layouts: 15.3 us -> 19.4 us
    dot_general x2, matrix products: 9.11 us -> 12.7 us  [apply_operator(): jnp.einsum('lbnr,lrbp->nbp', stacked, basis_tiles, preferred_element_type...]
  transfers between devices with their start and end apart: 8 -> 8, of which waited for: 6 -> 6; matrix products, arithmetic and copies ran while one was open for 4% -> 6% of each run, Pallas kernels for 0% -> 0%
where the time goes in v1:
time: 245 us; the launch traced here: 244 us
  blocking collectives  101 us (41%)
  local copies, waits for them, and re-layouts  54.7 us (22%)
  waiting for transfers between devices  31.2 us (13%)
  matrix products  28.7 us (12%)
  other arithmetic  26.8 us (11%)
    psum x2, blocking collectives, squares(): return lax.psum(jnp.sum(values * values, axis=1), 'leaf')  66.5 us
    all_gather x2, blocking collectives, on_device(): parts = lax.all_gather(x, 'leaf')  34.6 us
    ppermute x8, waiting for transfers between devices, from_partner(): lax.ppermute(array, axis, [(i, i ^ 1 << stride) for i in range(lax.axis_s...  31.2 us
    unnamed x35, local copies, waits for them, and re-layouts  19.4 us
    gather x2, local copies, waits for them, and re-layouts, on_device(): ordered = jnp.take(right_side, local_order, axis=1)  16.1 us
    scatter x1, other arithmetic, on_device(): field_solution = jnp.zeros_like(solution).at[:, local_order].set(solution)  14.8 us
    dot_general x2, matrix products, apply_operator(): jnp.einsum('lbnr,lrbp->nbp', stacked, basis_tiles, preferred_element_type...  12.7 us
    scatter x1, local copies, waits for them, and re-layouts, on_device(): field_residual = jnp.zeros_like(residual).at[:, local_order].set(residual)  12.5 us
  transfers between devices with their start and end apart: 8, of which 6 were waited for; matrix products, arithmetic and copies ran while one was open for 6% of the time, Pallas kernels for 0%

profile of v1, /device:TPU:0, one launch (start us, length us, event | category | flops | bytes accessed | tf_op | source)
XLA Modules:
  0.0 244.4 jit_solution(6603786406199990851)
XLA Ops:
  0.6 0.7 compare_and_fusion
  1.4 1.9 copy.24
  3.3 14.2 %gather_fusion = f32[4096,128]{1,0:T(8,128)} fusion(f32[128,4096]{0,1:T(8,128)S(1)} %copy.24, s32[4096]{0:T(1024)S(1)} %broadcast_clamp_fusion), kind=kCustom, calls=%fused_computation | custom fusion | bytes 4210688 | tf_op jit(solution)/shard_map/jit(_take)/gather | solution.py:75
  17.5 1.9 copy.25
  19.4 5.5 %fusion.25 = f32[8,7,128,128]{3,2,1,0:T(8,128)S(1)} fusion(bf16[7,16,8,8,512]{4,3,2,1,0:T(8,128)(2,1)} %bitcast.157, f32[128,8,512]{2,0,1:T(8,128)S(1)} %copy.25, pred[8,512]{1,0:T(8,128)(4,1)S(1)} %broadcast_in_dim.46), kind=kOutput, calls=%fused_computation.41 | convolution fusion | flops 940048384 | bytes 13111296 | tf_op jit(solution)/shard_map/nbp,lrbp->blnr/dot_general | solution.py:42
  25.1 0.5 collective-permute-start
  25.6 0.1 slice_reduce_fusion.3
  25.7 0.8 copy-done
  26.6 2.1 multiply_reduce_fusion.3
  28.8 0.8 constant_dynamic-update-slice_fusion.1
  29.7 2.2 fusion.47
  31.9 0.8 constant_dynamic-update-slice_fusion
  32.6 35.0 %psum.14 = f32[128]{0:T(128)S(1)} all-reduce(f32[128]{0:T(128)S(1)} %multiply_reduce_fusion.3), channel_id=1, replica_groups=mesh['groups'=2,'leaf'=16] {'leaf'}, use_global_device_ids=true, to_apply=%region_1.2 | all-reduce | flops 128 | bytes 1024 | tf_op jit(solution)/shard_map/psum | solution.py:68
  67.6 0.7 broadcast_dynamic-update-slice_fusion.9
  68.6 0.7 broadcast_dynamic-update-slice_fusion.8
  69.3 4.9 %collective-permute-done.1 = f32[3,128,128]{2,1,0:T(8,128)S(1)} collective-permute-done((f32[3,128,128]{2,1,0:T(8,128)S(1)}, f32[3,128,128]{2,1,0:T(8,128)S(1)}, u32[]{:S(2)}, u32[]{:S(2)}) %collective-permute-start.1) | collective-permute-done | bytes 196640 | tf_op jit(solution)/shard_map/ppermute | solution.py:11
  74.3 5.4 %collective-permute-done.2 = f32[2,128,128]{2,1,0:T(8,128)S(1)} collective-permute-done((f32[2,128,128]{2,1,0:T(8,128)S(1)}, f32[2,128,128]{2,1,0:T(8,128)S(1)}, u32[]{:S(2)}, u32[]{:S(2)}) %collective-permute-start.2) | collective-permute-done | bytes 131104 | tf_op jit(solution)/shard_map/ppermute | solution.py:11
  79.8 0.7 broadcast_dynamic-update-slice_fusion.7
  80.6 4.4 %collective-permute-done.3 = f32[1,128,128]{2,1,0:T(8,128)S(1)} collective-permute-done((f32[1,128,128]{2,1,0:T(8,128)S(1)}, f32[1,128,128]{2,1,0:T(8,128)S(1)}, u32[]{:S(2)}, u32[]{:S(2)}) %collective-permute-start.3) | collective-permute-done | bytes 65568 | tf_op jit(solution)/shard_map/ppermute | solution.py:11
  85.0 0.7 broadcast_dynamic-update-slice_fusion.6
  85.7 0.7 broadcast_dynamic-update-slice_fusion.5
  86.5 6.4 %multiply_reduce_fusion.2 = (f32[128]{0:T(128)S(1)}, f32[128,8,512]{2,0,1:T(8,128)}) fusion(f32[128,8,512]{2,0,1:T(8,128)S(1)} %copy.25, pred[8,512]{1,0:T(8,128)(4,1)S(1)} %broadcast_in_dim.46, f32[8,128,512]{2,1,0:T(8,128)S(1)} %copy-done.8, bf16[7,8,128,128]{3,2,0,1:T(8,128)(2,1)} %broadcast_dynamic-update-slice_fusion.5, ...), kind=kOutput, calls=%fused_computation.39 | convolution fusion | flops 941621120 | bytes 15471104 | tf_op jit(solution)/shard_map/lbnr,lrbp->nbp/dot_general | solution.py:61
  92.8 17.1 %all-gather.2 = f32[16,1,128]{2,1,0:T(1,128)S(1)} all-gather(f32[1,1,128]{2,1,0:T(1,128)S(1)} %bitcast.171), channel_id=2, replica_groups=mesh['groups'=2,'leaf'=16] {'leaf'}, dimensions={0}, use_global_device_ids=true | all-gather | bytes 8704 | tf_op jit(solution)/shard_map/all_gather | solution.py:85
  110.0 2.1 multiply_reduce_fusion.1
  112.1 31.5 %psum.15 = f32[128]{0:T(128)S(1)} all-reduce(f32[128]{0:T(128)S(1)} %multiply_reduce_fusion.1), channel_id=1, replica_groups=mesh['groups'=2,'leaf'=16] {'leaf'}, use_global_device_ids=true, to_apply=%region_9.10 | all-reduce | flops 128 | bytes 1024 | tf_op jit(solution)/shard_map/psum | solution.py:68
  143.6 2.2 multiply_add_fusion
  145.8 6.3 %fusion.28 = f32[8,7,128,128]{3,2,1,0:T(8,128)S(1)} fusion(bf16[7,16,8,8,512]{4,3,2,1,0:T(8,128)(2,1)} %bitcast.159, f32[128,8,512]{2,0,1:T(8,128)S(1)} %multiply_add_fusion), kind=kOutput, calls=%fused_computation.42 | convolution fusion | flops 940048384 | bytes 13107200 | tf_op jit(solution)/shard_map/nbp,lrbp->blnr/dot_general | solution.py:42
  152.3 2.0 copy-done.6
  154.2 2.0 fusion.45
  156.4 0.7 constant_dynamic-update-slice_fusion.3
  157.2 0.8 constant_dynamic-update-slice_fusion.2
  158.0 1.8 copy.30
  159.8 0.7 broadcast_dynamic-update-slice_fusion.4
  160.7 0.7 broadcast_dynamic-update-slice_fusion.3
  161.5 6.6 %collective-permute-done.5 = f32[3,128,128]{2,1,0:T(8,128)S(1)} collective-permute-done((f32[3,128,128]{2,1,0:T(8,128)S(1)}, f32[3,128,128]{2,1,0:T(8,128)S(1)}, u32[]{:S(2)}, u32[]{:S(2)}) %collective-permute-start.5) | collective-permute-done | bytes 196640 | tf_op jit(solution)/shard_map/ppermute | solution.py:11
  168.2 5.1 %collective-permute-done.6 = f32[2,128,128]{2,1,0:T(8,128)S(1)} collective-permute-done((f32[2,128,128]{2,1,0:T(8,128)S(1)}, f32[2,128,128]{2,1,0:T(8,128)S(1)}, u32[]{:S(2)}, u32[]{:S(2)}) %collective-permute-start.6) | collective-permute-done | bytes 131104 | tf_op jit(solution)/shard_map/ppermute | solution.py:11
  173.4 0.7 broadcast_dynamic-update-slice_fusion.2
  174.1 4.8 %collective-permute-done.7 = f32[1,128,128]{2,1,0:T(8,128)S(1)} collective-permute-done((f32[1,128,128]{2,1,0:T(8,128)S(1)}, f32[1,128,128]{2,1,0:T(8,128)S(1)}, u32[]{:S(2)}, u32[]{:S(2)}) %collective-permute-start.7) | collective-permute-done | bytes 65568 | tf_op jit(solution)/shard_map/ppermute | solution.py:11
  179.0 0.7 broadcast_dynamic-update-slice_fusion.1
  179.7 0.7 broadcast_dynamic-update-slice_fusion
  180.5 6.4 %multiply_reduce_fusion = (f32[128]{0:T(128)S(1)}, f32[128,8,512]{2,0,1:T(8,128)}) fusion(f32[128,8,512]{2,0,1:T(8,128)S(1)} %copy-done.3, f32[8,128,512]{2,1,0:T(8,128)S(1)} %copy-done.7, bf16[7,8,128,128]{3,2,0,1:T(8,128)(2,1)} %broadcast_dynamic-update-slice_fusion, bf16[7,16,8,8,512]{4,3,2,1,0:T(8,128)(2,1)} %bitcast.160), kind=kOutput, calls=%fused_computation.34 | convolution fusion | flops 941096832 | bytes 15467008 | tf_op jit(solution)/shard_map/lbnr,lrbp->nbp/dot_general | solution.py:61
  186.8 17.5 %all-gather.3 = f32[16,1,128]{2,1,0:T(1,128)S(1)} all-gather(f32[1,1,128]{2,1,0:T(1,128)S(1)} %bitcast.170), channel_id=3, replica_groups=mesh['groups'=2,'leaf'=16] {'leaf'}, dimensions={0}, use_global_device_ids=true | all-gather | bytes 8704 | tf_op jit(solution)/shard_map/all_gather | solution.py:85
  204.3 3.1 %copy.31 = f32[128,8,512]{0,2,1:T(8,128)} copy(f32[128,8,512]{2,0,1:T(8,128)} %get-tuple-element.32) | data formatting | bytes 4194304 | tf_op jit(solution)/shard_map/add | solution.py:64
  207.4 3.9 %fusion.14 = (f32[128,4096]{0,1:T(8,128)}, f32[128,4096]{0,1:T(8,128)}) fusion(f32[128,8,512]{0,2,1:T(8,128)} %copy.31, f32[128]{0:T(128)S(1)} %div.11, f32[128,8,512]{0,2,1:T(8,128)} %copy.30, f32[128]{0:T(128)S(1)} %div.9, f32[4096,128]{1,0:T(8,128)S(1)} %copy-done.1, pred[4096]{0:T(1024)(128)(4,1)S(1)} %get-tuple-element.10), kind=kLoop, calls=%fused_computation.20 | loop fusion | flops 2621440 | bytes 10490880 | tf_op jit(solution)/shard_map/sub | solution.py:89
  211.3 12.5 %scatter_custom_fusion.1 = f32[128,4096]{0,1:T(8,128)} fusion(s32[4096]{0:T(1024)S(1)} %get-tuple-element.11, f32[128,4096]{0,1:T(8,128)} %get-tuple-element.8, f32[]{:T(128)} %constant.13.clone.1), kind=kCustom, calls=%fused_computation.17 | custom fusion | bytes 4194308 | tf_op jit(solution)/shard_map/scatter | solution.py:95
  223.8 2.9 %copy.33 = f32[128,4096]{1,0:T(8,128)} copy(f32[128,4096]{0,1:T(8,128)} %scatter_custom_fusion.1) | data formatting | bytes 4194304
  226.7 14.8 %scatter_custom_fusion = f32[128,4096]{0,1:T(8,128)} fusion(s32[4096]{0:T(1024)S(1)} %get-tuple-element.11, f32[128,4096]{0,1:T(8,128)} %get-tuple-element.9, f32[4096,128]{1,0:T(8,128)S(1)} %copy-done.1, f32[128]{0:T(128)S(1)} %div.10, f32[128]{0:T(128)S(1)} %div.11, f32[128]{0:T(128)S(1)} %div.9, f32[]{:T(128)} %constant.18.clone.1, ...), kind=kCustom, calls=%fused_computation.21 | custom fusion | flops 3145728 | bytes 6297096 | tf_op jit(solution)/shard_map/scatter | solution.py:94
  241.5 2.9 %copy.32 = f32[128,4096]{1,0:T(8,128)} copy(f32[128,4096]{0,1:T(8,128)} %scatter_custom_fusion) | data formatting | bytes 4194304
  (70 shorter events, 1.5 us)
Async XLA Ops:
  25.0 1.6 copy-start
  25.1 3.6 %copy-start.9 = (f32[7,128]{1,0:T(8,128)S(1)}, f32[7,128]{1,0:T(8,128)}, u32[]{:S(2)}) copy-start(f32[7,128]{1,0:T(8,128)} %param.9) | copy-start | bytes 10756
  25.1 43.3 %collective-permute-start = (f32[4,128,128]{2,1,0:T(8,128)S(1)}, f32[4,128,128]{2,1,0:T(8,128)S(1)}, u32[]{:S(2)}, u32[]{:S(2)}) collective-permute-start(f32[4,128,128]{2,1,0:T(8,128)S(1)} %slice_reduce_fusion.1), channel_id=1, source_target_pairs={{0,1},{1,0},{2,3},{3,2},{4,5},{5,4},{6,7},{7,6},{8,9},{9,8},{10,11... | collective-permute-start | bytes 786440 | tf_op jit(solution)/shard_map/ppermute | solution.py:11
  26.6 3.1 %copy-start.5 = (bf16[8,512,512]{2,1,0:T(8,128)(2,1)S(1)}, bf16[8,512,512]{2,1,0:T(8,128)(2,1)}, u32[]{:S(2)}) copy-start(bf16[8,512,512]{2,1,0:T(8,128)(2,1)} %param.7) | copy-start | bytes 12582916
  68.4 18.1 %copy-start.8 = (f32[8,128,512]{2,1,0:T(8,128)S(1)}, f32[8,128,512]{2,1,0:T(8,128)}, u32[]{:S(2)}) copy-start(f32[8,128,512]{2,1,0:T(8,128)} %fusion.47) | copy-start | bytes 6291460
  68.5 5.7 %collective-permute-start.1 = (f32[3,128,128]{2,1,0:T(8,128)S(1)}, f32[3,128,128]{2,1,0:T(8,128)S(1)}, u32[]{:S(2)}, u32[]{:S(2)}) collective-permute-start(f32[3,128,128]{2,1,0:T(8,128)S(1)} %slice.122), channel_id=1, source_target_pairs={{0,2},{1,3},{2,0},{3,1},{4,6},{5,7},{6,4},{7,5},{8,10},{9,11},{10,... | collective-permute-start | bytes 589832 | tf_op jit(solution)/shard_map/ppermute | solution.py:11
  74.2 5.5 %collective-permute-start.2 = (f32[2,128,128]{2,1,0:T(8,128)S(1)}, f32[2,128,128]{2,1,0:T(8,128)S(1)}, u32[]{:S(2)}, u32[]{:S(2)}) collective-permute-start(f32[2,128,128]{2,1,0:T(8,128)S(1)} %slice.124), channel_id=1, source_target_pairs={{0,4},{1,5},{2,6},{3,7},{4,0},{5,1},{6,2},{7,3},{8,12},{9,13},{10,... | collective-permute-start | bytes 393224 | tf_op jit(solution)/shard_map/ppermute | solution.py:11
  79.8 5.2 %collective-permute-start.3 = (f32[1,128,128]{2,1,0:T(8,128)S(1)}, f32[1,128,128]{2,1,0:T(8,128)S(1)}, u32[]{:S(2)}, u32[]{:S(2)}) collective-permute-start(f32[1,128,128]{2,1,0:T(8,128)S(1)} %slice.126), channel_id=1, source_target_pairs={{0,8},{1,9},{2,10},{3,11},{4,12},{5,13},{6,14},{7,15},{8,0},{9,1},... | collective-permute-start | bytes 196616 | tf_op jit(solution)/shard_map/ppermute | solution.py:11
  145.8 6.5 %copy-start.2 = (f32[128,8,512]{2,0,1:T(8,128)}, f32[128,8,512]{2,0,1:T(8,128)S(1)}, u32[]{:S(2)}) copy-start(f32[128,8,512]{2,0,1:T(8,128)S(1)} %multiply_add_fusion) | copy-start | bytes 6291460
  152.0 2.2 copy-start.6
  156.3 1.7 copy-start.4
  156.3 4.3 %collective-permute-start.4 = (f32[4,128,128]{2,1,0:T(8,128)S(1)}, f32[4,128,128]{2,1,0:T(8,128)S(1)}, u32[]{:S(2)}, u32[]{:S(2)}) collective-permute-start(f32[4,128,128]{2,1,0:T(8,128)S(1)} %slice_reduce_fusion), channel_id=1, source_target_pairs={{0,1},{1,0},{2,3},{3,2},{4,5},{5,4},{6,7},{7,6},{8,9},{9,8},{10,11... | collective-permute-start | bytes 786440 | tf_op jit(solution)/shard_map/ppermute | solution.py:11
  160.6 19.9 %copy-start.3 = (f32[128,8,512]{2,0,1:T(8,128)S(1)}, f32[128,8,512]{2,0,1:T(8,128)}, u32[]{:S(2)}) copy-start(f32[128,8,512]{2,0,1:T(8,128)} %copy-done.2) | copy-start | bytes 6291460
  160.6 19.9 %copy-start.7 = (f32[8,128,512]{2,1,0:T(8,128)S(1)}, f32[8,128,512]{2,1,0:T(8,128)}, u32[]{:S(2)}) copy-start(f32[8,128,512]{2,1,0:T(8,128)} %fusion.45) | copy-start | bytes 6291460
  160.7 7.4 %collective-permute-start.5 = (f32[3,128,128]{2,1,0:T(8,128)S(1)}, f32[3,128,128]{2,1,0:T(8,128)S(1)}, u32[]{:S(2)}, u32[]{:S(2)}) collective-permute-start(f32[3,128,128]{2,1,0:T(8,128)S(1)} %slice.132), channel_id=1, source_target_pairs={{0,2},{1,3},{2,0},{3,1},{4,6},{5,7},{6,4},{7,5},{8,10},{9,11},{10,... | collective-permute-start | bytes 589832 | tf_op jit(solution)/shard_map/ppermute | solution.py:11
  168.1 5.2 %collective-permute-start.6 = (f32[2,128,128]{2,1,0:T(8,128)S(1)}, f32[2,128,128]{2,1,0:T(8,128)S(1)}, u32[]{:S(2)}, u32[]{:S(2)}) collective-permute-start(f32[2,128,128]{2,1,0:T(8,128)S(1)} %slice.134), channel_id=1, source_target_pairs={{0,4},{1,5},{2,6},{3,7},{4,0},{5,1},{6,2},{7,3},{8,12},{9,13},{10,... | collective-permute-start | bytes 393224 | tf_op jit(solution)/shard_map/ppermute | solution.py:11
  173.3 5.7 %collective-permute-start.7 = (f32[1,128,128]{2,1,0:T(8,128)S(1)}, f32[1,128,128]{2,1,0:T(8,128)S(1)}, u32[]{:S(2)}, u32[]{:S(2)}) collective-permute-start(f32[1,128,128]{2,1,0:T(8,128)S(1)} %slice.136), channel_id=1, source_target_pairs={{0,8},{1,9},{2,10},{3,11},{4,12},{5,13},{6,14},{7,15},{8,0},{9,1},... | collective-permute-start | bytes 196616 | tf_op jit(solution)/shard_map/ppermute | solution.py:11
  204.3 3.1 %copy-start.1 = (f32[4096,128]{1,0:T(8,128)S(1)}, f32[4096,128]{1,0:T(8,128)}, u32[]{:S(2)}) copy-start(f32[4096,128]{1,0:T(8,128)} %gather_fusion) | copy-start | bytes 6291460
